TPU v7x, 256 devices: a whole 4x4x8 slice. The times are simulated.
256 devices in a mesh: tok: 32 (over x, y, z_hi), blk: 8 (over z_lo, core).
Axes of the slice: x: 4, y: 4, z: 8 (z_hi: 2, z_lo: 4; z = z_hi * 4 + z_lo), core: 2. Of those that a mesh axis runs over, the one named last changes fastest.
Arguments:
- activations: bfloat16 [2048, 4096], P('tok', 'blk'), may hold values from -40 to 40
- gradients: bfloat16 [2048, 14336], P('tok', 'blk'), may hold values from -40 to 40
- input_basis: bfloat16 [4096, 4096], P('tok', 'blk'), may hold values from -0.09375 to 0.09375
- output_basis: bfloat16 [14336, 14336], P('blk', 'tok'), may hold values from -0.046875 to 0.046875
Outputs:
- input_covariance: float32 [4096, 4096], P('blk', 'tok')
- output_covariance: float32 [14336, 14336], P('blk', 'tok')
- corrections: float32 [4096, 14336], P('blk', 'tok')
All inputs are finite; a program needn't handle non-finite values.
Results may differ from a plain program's by a relative error of at most 0.00046.
Values may be sent and summed in bfloat16 or wider, within the bound.
No kernel may reach another device: no remote copies, remote signals or barrier semaphores. Data moves between devices by JAX's collectives and lax.ppermute only.
A program may use at most 128 MiB of HBM per device.

v0:
```python
import jax
import jax.numpy as jnp
from jax import lax
from jax.sharding import PartitionSpec as P


def spread(block, axis, source):
    block = jnp.where(lax.axis_index(axis) == source, block, jnp.zeros_like(block))
    return lax.psum(block, axis)


def cross_product(left, right):
    return lax.dot_general(
        left, right, (((0,), (0,)), ((), ())), preferred_element_type=jnp.float32
    )


def local(activations, gradients, input_basis, output_basis):
    act_panel, grad_panel = (
        lax.all_gather(activations, "tok", axis=0, tiled=True),
        lax.all_gather(gradients, "tok", axis=0, tiled=True),
    )
    per_owner = lax.axis_size("tok") // lax.axis_size("blk")
    tok_index = lax.axis_index("tok")
    owner_index = tok_index // per_owner
    sub_index = tok_index % per_owner
    act_width = act_panel.shape[1] // per_owner
    grad_width = grad_panel.shape[1] // per_owner
    act_piece = lax.dynamic_slice_in_dim(act_panel, sub_index * act_width, act_width, 1)
    grad_piece = lax.dynamic_slice_in_dim(grad_panel, sub_index * grad_width, grad_width, 1)
    act_side, grad_side = (
        spread(act_piece, "blk", owner_index),
        spread(grad_piece, "blk", owner_index),
    )
    total_rows = act_panel.shape[0]
    image_terms = jnp.dot(grad_panel, output_basis, preferred_element_type=jnp.float32)
    feature_terms = jnp.dot(act_side, input_basis, preferred_element_type=jnp.float32)
    projected_out = lax.psum(image_terms, "blk")
    projected_in = lax.psum(feature_terms, "tok")
    out_squares = (projected_out * projected_out).astype(jnp.bfloat16)
    in_squares = (projected_in * projected_in).astype(jnp.bfloat16)
    input_covariance = cross_product(act_panel, act_side) / total_rows
    output_covariance = cross_product(grad_panel, grad_side) / total_rows
    corrections = cross_product(in_squares, out_squares) / total_rows
    return (input_covariance, output_covariance, corrections)


def solution(mesh):
    placed = (P("tok", "blk"), P("tok", "blk"), P("tok", "blk"), P("blk", "tok"))
    return jax.shard_map(
        local,
        mesh=mesh,
        in_specs=placed,
        out_specs=(P("blk", "tok"), P("blk", "tok"), P("blk", "tok")),
        check_vma=False,
    )
```

profile of v0, /device:TPU:96, one launch (start us, length us, event | category | flops | bytes accessed | tf_op | source)
XLA Modules:
  0.0 983.8 jit_solution(9974383799997621214)
XLA Ops:
  7.2 0.0 all-gather.3.cloned.1.call-start
  7.2 0.7 all-gather.3.cloned.1.call-update
  7.9 0.0 all-gather.5.cloned.1.call-start
  8.0 0.7 all-gather.5.cloned.1.call-update
  8.7 0.0 all-reduce.9.cloned.1.call-start
  8.7 92.8 %all-gather.3.cloned.1.call-done = bf16[2048,512]{1,0:T(8,128)(2,1)} async-done(((bf16[64,512]{1,0:T(8,128)(2,1)}), bf16[2048,512]{1,0:T(8,128)(2,1)}) %all-gather.3.cloned.1.call-update) | async-done | bytes 2097168 | tf_op jit(solution)/shard_map/all_gather | solution.py:20
  101.6 1.9 dynamic-slice_select_fusion.1
  103.5 135.5 %all-gather.5.cloned.1.call-done = bf16[2048,1792]{1,0:T(8,128)(2,1)} async-done(((bf16[64,1792]{1,0:T(8,128)(2,1)}), bf16[2048,1792]{1,0:T(8,128)(2,1)}) %all-gather.5.cloned.1.call-update) | async-done | bytes 7340048 | tf_op jit(solution)/shard_map/all_gather | solution.py:21
  239.0 4.4 dynamic-slice_select_fusion
  243.4 0.0 all-reduce.9.cloned.1.call-update
  243.4 0.0 all-reduce.7.cloned.1.call-start
  243.5 8.8 fusion.4
  252.3 0.0 all-reduce.7.cloned.1.call-update
  252.3 0.0 all-reduce.5.cloned.1.call-start
  252.3 73.3 %all-reduce.9.cloned.1.call-done = (bf16[2048,128]{1,0:T(8,128)(2,1)}, bf16[2048,448]{1,0:T(8,128)(2,1)}) async-done(((bf16[2048,128]{1,0:T(8,128)(2,1)}, bf16[2048,448]{1,0:T(8,128)(2,1)}), (bf16[2048,128]{1,0:T(8,128)(2,1)}, bf16[2048,448]{1,0:T(8,128)(2,1)})) %all-reduce.9.cloned.1.call-update) | async-done | bytes 2359312 | tf_op jit(solution)/shard_map/psum | solution.py:9
  325.6 3.7 fusion.3
  329.3 0.0 all-reduce.5.cloned.1.call-update
  329.3 1.0 copy-done.1
  330.3 2.1 fusion.2
  332.4 0.8 copy.7
  333.2 9.0 multiply_bitcast_fusion
  342.2 95.3 %all-reduce.7.cloned.1.call-done = f32[2048,448]{1,0:T(8,128)} async-done(((f32[2048,448]{1,0:T(8,128)}), f32[2048,448]{1,0:T(8,128)}) %all-reduce.7.cloned.1.call-update) | async-done | bytes 3670032 | tf_op jit(solution)/shard_map/psum | solution.py:38
  437.5 534.2 %all-reduce.5.cloned.1.call-done = f32[2048,512]{1,0:T(8,128)} async-done(((f32[2048,512]{1,0:T(8,128)}), f32[2048,512]{1,0:T(8,128)}) %all-reduce.5.cloned.1.call-update) | async-done | bytes 4194320 | tf_op jit(solution)/shard_map/psum | solution.py:39
  971.7 5.6 fusion.1
  (5 shorter events, 0.0 us)
Async XLA Ops:
  7.2 236.3 %copy-start = (bf16[1792,448]{0,1:T(8,128)(2,1)S(1)}, bf16[1792,448]{0,1:T(8,128)(2,1)}, u32[]{:S(2)}) copy-start(bf16[1792,448]{0,1:T(8,128)(2,1)} %param.7) | copy-start | bytes 4816900
  7.2 94.4 %all-gather.3.cloned.1.call-start = ((), (), s32[]{:S(2)}) async-start(), calls=%async_computation | async-start | bytes 2162688 | tf_op jit(solution)/shard_map/all_gather | solution.py:20
  7.9 231.1 %all-gather.5.cloned.1.call-start = ((), (), s32[]{:S(2)}) async-start(), calls=%async_computation.1 | async-start | bytes 7569408 | tf_op jit(solution)/shard_map/all_gather | solution.py:21
  8.7 316.9 %all-reduce.9.cloned.1.call-start = ((), (), s32[]{:S(2)}) async-start(), calls=%async_computation.4 | async-start | bytes 5242880 | tf_op jit(solution)/shard_map/psum | solution.py:9
  243.4 194.1 %all-reduce.7.cloned.1.call-start = ((), (), s32[]{:S(2)}) async-start(), calls=%async_computation.3 | async-start | bytes 8388608 | tf_op jit(solution)/shard_map/psum | solution.py:38
  252.3 73.3 %copy-start.2 = (bf16[128,512]{1,0:T(8,128)(2,1)S(1)}, bf16[128,512]{1,0:T(8,128)(2,1)}, u32[]{:S(2)}) copy-start(bf16[128,512]{1,0:T(8,128)(2,1)} %param.6) | copy-start | bytes 393220
  252.3 719.5 %all-reduce.5.cloned.1.call-start = ((), (), s32[]{:S(2)}) async-start(), calls=%async_computation.2 | async-start | bytes 8388608 | tf_op jit(solution)/shard_map/psum | solution.py:39
  329.3 1.0 copy-start.1
Sparse Core Ops, SparseCore 0:
  11.4 90.0 all-gather.2
  105.0 134.0 all-gather.4
  243.6 81.9 all-reduce.8
  328.1 109.3 all-reduce.6
  440.0 531.6 all-reduce.4
where the time goes:
time: 984 us
  waiting for transfers between devices  933 us (95%)
  matrix products  29 us (3%)
  between operations  13.8 us (1%)
    psum x1, waiting for transfers between devices, local(): projected_in = lax.psum(feature_terms, 'tok')  534 us
    all_gather x1, waiting for transfers between devices, local(): lax.all_gather(gradients, 'tok', axis=0, tiled=True)  136 us
    psum x1, waiting for transfers between devices, local(): projected_out = lax.psum(image_terms, 'blk')  95.3 us
    all_gather x1, waiting for transfers between devices, local(): lax.all_gather(activations, 'tok', axis=0, tiled=True)  92.8 us
    psum x1, waiting for transfers between devices, spread(): return lax.psum(block, axis)  73.3 us
  transfers between devices with their start and end apart: 5, of which 5 were waited for; matrix products, arithmetic and copies ran while one was open for 3% of the time, Pallas kernels for 0%

commit v1 on v0

v1 whole, which is shorter than its diff:
```python
import functools

import jax
import jax.numpy as jnp
from jax import lax
from jax.experimental import pallas as pl
from jax.experimental.pallas import tpu as pltpu
from jax.sharding import Mesh
from jax.sharding import PartitionSpec as P

AXES = ("x", "y", "h", "l", "c")
SIZES = (4, 4, 2, 4, 2)
RING = 4


def after(value, *others):
    return lax.optimization_barrier((value, others))[0]


def swap(block, axis, bit):
    size = SIZES[AXES.index(axis)]
    return lax.ppermute(block, axis, [(i, i ^ bit) for i in range(size)])


def turn(block, axis, step):
    return lax.ppermute(block, axis, [(i, (i + step) % RING) for i in range(RING)])


def line(block, step):
    return lax.ppermute(block, "l", [(i, i + step) for i in range(RING) if 0 <= i + step < RING])


def copies(moves, out_shapes, *operands):
    count = len(moves(0, 0))

    def kernel(*refs):
        ins, outs, sems = refs[: len(operands)], refs[len(operands) : -1], refs[-1]
        started = [
            pltpu.make_async_copy(ins[i].at[at], outs[o].at[to], sems.at[n])
            for n, (i, at, o, to) in enumerate(moves(lax.axis_index("x"), lax.axis_index("y")))
        ]
        for copy in started:
            copy.start()
        for copy in started:
            copy.wait()

    dtype = operands[0].dtype
    total = sum(functools.reduce(lambda a, b: a * b, shape) for shape in out_shapes) * 2
    return pl.pallas_call(
        kernel,
        out_shape=[jax.ShapeDtypeStruct(shape, dtype) for shape in out_shapes],
        in_specs=[pl.BlockSpec(memory_space=pl.ANY)] * len(operands),
        out_specs=[pl.BlockSpec(memory_space=pltpu.VMEM)] * len(out_shapes),
        scratch_shapes=[pltpu.SemaphoreType.DMA((count,))],
        compiler_params=pltpu.CompilerParams(vmem_limit_bytes=2 * total + (4 << 20)),
        cost_estimate=pl.CostEstimate(flops=0, bytes_accessed=2 * total, transcendentals=0),
    )(*operands)


def near(block, axis):
    return turn(block, axis, -1), turn(block, axis, 1)


def halves(following, previous):
    rows, cols = following.shape
    half = rows // 2

    def moves(x, y):
        return [
            (0, pl.ds(0, half), 0, pl.ds(0, half)),
            (1, pl.ds(half, half), 1, pl.ds(0, half)),
        ]

    return copies(moves, [(half, cols)] * 2, previous, following)


def opposite(upper, lower, axis):
    return turn(upper, axis, 1), turn(lower, axis, -1)


def first_ring(blocks, along_y):
    size, cols = blocks[0].shape

    def moves(x, y):
        place = y if along_y else x
        at = [lax.rem(place + step, RING) * size for step in range(RING)]
        spans = ((at[0], size), (at[1], size), (at[2], size // 2), (at[2] + size // 2, size // 2), (at[3], size))
        return [(i, pl.ds(0, length), 0, pl.ds(start, length)) for i, (start, length) in enumerate(spans)]

    return copies(moves, [(4 * size, cols)], *blocks)[0]


def second_rings(a_blocks, b_blocks):
    size, cols = a_blocks[0].shape[0] // 4, a_blocks[0].shape[1]

    def moves(x, y):
        first, found = lax.axis_index("c"), []
        for n, place in enumerate((y, x)):
            base = lax.rem(first + n, 2) * 16
            for i, (step, parts) in enumerate(((0, range(4)), (1, range(4)), (2, (0, 1)), (2, (2, 3)), (3, range(4)))):
                outer = lax.rem(place + step, RING)
                for k, inner in enumerate(parts):
                    at = base + (inner * 4 + outer if n == 0 else outer * 4 + inner)
                    found.append((5 * n + i, pl.ds(k * size, size), 0, pl.ds(at * size, size)))
        return found

    return copies(moves, [(32 * size, cols)], *a_blocks, *b_blocks)[0]


def pick(rows, bit):
    half = rows.shape[0] // 2
    return (
        lax.dynamic_slice_in_dim(rows, bit * half, half),
        lax.dynamic_slice_in_dim(rows, (1 - bit) * half, half),
    )


def join(mine, other, bit):
    return jnp.where(bit == 0, jnp.concatenate([mine, other]), jnp.concatenate([other, mine]))


def swap_half(rows, exponent, axis, bit, mask):
    mine, other = pick(rows, bit)
    sent = (other * jnp.exp2(13.0 - exponent)).astype(jnp.float16)
    got = swap(sent, axis, mask), swap(jnp.full((8, 128), exponent), axis, mask)
    return mine, sent, got


def add_half(mine, got, exponent):
    rows, theirs = got
    theirs = theirs[0, 0]
    return mine + rows.astype(jnp.float32) * jnp.exp2(theirs - 13.0), jnp.maximum(exponent, theirs) + 1.0


def matmul(left, right):
    return jnp.dot(left, right, preferred_element_type=jnp.float32)


def cross_product(left, right):
    return lax.dot_general(
        left, right, (((0,), (0,)), ((), ())), preferred_element_type=jnp.float32
    )


def local(activations, gradients, input_basis, output_basis):
    x, y, h, l, c = (lax.axis_index(axis) for axis in AXES)
    rows, act_width = activations.shape
    grad_width = gradients.shape[1]
    total_rows = rows * 32
    grad_part, act_part = grad_width // 4, act_width // 4
    part = grad_part + act_part

    partner = swap(gradients, "h", 1)
    partner_acts = swap(activations, "h", 1)
    basis = lax.all_gather(input_basis, ("x", "y"), axis=0, tiled=True)
    a_next, a_prev = near(gradients, "x")
    a_up, a_down = opposite(*halves(a_next, a_prev), "x")
    b_next, b_prev = near(partner, "y")

    def wanted(grads, acts, j):
        return [
            lax.dynamic_slice_in_dim(grads, (2 * j + h) * grad_part, grad_part, 1),
            lax.dynamic_slice_in_dim(acts, (2 * j + h) * act_part, act_part, 1),
        ]

    lines = jnp.stack(
        [
            jnp.concatenate(wanted(grads, acts, j), axis=1)
            for grads, acts in ((gradients, activations), (partner, partner_acts))
            for j in range(2)
        ]
    )[None]
    lines = after(lines, a_next, a_prev)
    lines = join(lines, after(swap(lines, "l", 1), b_next, b_prev), l & 1)
    b_up, b_down = opposite(*halves(b_next, b_prev), "y")
    a_up, a_down = after((a_up, a_down), lines)
    first_a = first_ring((gradients, a_next, a_up, a_down, a_prev), False)
    first_b = first_ring((partner, b_next, b_up, b_down, b_prev), True)
    first_a, first_b = lax.optimization_barrier((first_a, first_b))
    a_next, a_prev = near(first_a, "y")
    b_next, b_prev = near(first_b, "x")
    a_halves, b_halves = halves(a_next, a_prev), halves(b_next, b_prev)
    a_up, a_down = opposite(*a_halves, "y")
    b_up, b_down = opposite(*b_halves, "x")
    other_lines = after(swap(lines, "l", 2), a_halves, b_halves)
    lines = join(lines, other_lines, l >> 1).reshape(4, 2, 2, rows, part)

    mine = lax.dynamic_index_in_dim(lines, c, 1, keepdims=False)
    other = swap(lax.dynamic_index_in_dim(lines, 1 - c, 1, keepdims=False), "c", 1)
    sides = jnp.where(c == 0, jnp.stack([mine, other], 1), jnp.stack([other, mine], 1))
    sides = sides.reshape(16, rows, part)

    act_rows = sides[:, :, grad_part:].transpose(1, 0, 2).reshape(rows, 16 * act_part)
    act_rows = jnp.concatenate([act_rows, swap(act_rows, "c", 1)])
    part_in = matmul(act_rows, basis)
    other_in = swap(part_in, "h", 1)

    grads = second_rings(
        (first_a, a_next, a_up, a_down, a_prev), (first_b, b_next, b_up, b_down, b_prev)
    )
    half = total_rows // 2
    part_out = matmul(after(grads[half:], part_in), output_basis)
    sums = matmul(after(grads[:half], part_out), output_basis)

    other_in = after(other_in, sums)
    projected_in = part_in + jnp.concatenate([other_in[rows:], other_in[:rows]])
    in_squares = (projected_in * projected_in).astype(jnp.bfloat16)
    shared = jnp.concatenate([in_squares, join(activations, partner_acts, c)], axis=1)

    sums += swap(part_out, "c", 1)
    exponent = jnp.ceil(jnp.log2(jnp.maximum(jnp.max(jnp.abs(sums)), 1e-30)))
    mine, sent, got = swap_half(sums, exponent, "l", l & 1, 1)
    shared = lax.all_gather(after(shared, sent), ("x", "y"), axis=0)
    shared = shared.reshape(16, 2, rows, 2 * act_width)
    sides = lax.all_to_all(after(sides, sent), ("x", "y"), 0, 0, tiled=True).reshape(half, part)
    sums, exponent = add_half(mine, got, exponent)
    mine, sent, got = swap_half(sums, exponent, "l", l >> 1, 2)
    sides = after(sides, sent)
    sides = jnp.concatenate([sides, swap(sides, "c", 1)])
    sums, _ = add_half(mine, after(got, sides), exponent)
    squares = (sums * sums).astype(jnp.bfloat16)
    other_squares = swap(squares, "l", 2)
    output_covariance = cross_product(grads, after(sides, squares)[:, :grad_part]) / total_rows
    squares = join(squares, after(other_squares, output_covariance), l >> 1)
    other_squares = swap(squares, "l", 1)
    shared = after(shared, squares)
    input_covariance = sum(
        cross_product(
            shared[:, i, :, act_width:].reshape(half, act_width),
            sides[i * half : (i + 1) * half, grad_part:],
        )
        for i in range(2)
    ) / total_rows
    in_squares = [shared[:, i, :, :act_width].reshape(half, act_width) for i in range(2)]
    other_squares = after(other_squares, input_covariance, *in_squares)
    squares = join(squares, other_squares, l & 1)
    other_squares = swap(squares, "c", 1)
    corrections = cross_product(in_squares[0], squares) + cross_product(in_squares[1], other_squares)
    return input_covariance, output_covariance, corrections / total_rows


def solution(mesh):
    fine = Mesh(mesh.devices.reshape(SIZES), AXES)
    tok, blk = ("x", "y", "h"), ("l", "c")
    return jax.shard_map(
        local,
        mesh=fine,
        in_specs=(P(tok, blk), P(tok, blk), P(tok, blk), P(blk, tok)),
        out_specs=(P(blk, tok), P(blk, tok), P(blk, tok)),
        check_vma=False,
    )
```

time: 984 us -> 231 us (0.23)
  the two profiles are of different devices: /device:TPU:96 before, /device:TPU:1 now
where the time goes in v1:
time: 231 us; the launch traced here: 230 us
  waiting for transfers between devices  76.5 us (33%)
  starting transfers between devices  66.6 us (29%)
  matrix products  26.4 us (11%)
  between operations  17.3 us (7%)
  local copies, waits for them, and re-layouts  15.9 us (7%)
  other arithmetic  15.3 us (7%)
  Pallas kernels  12.1 us (5%)
    ppermute x16, starting transfers between devices, swap(): return lax.ppermute(block, axis, [(i, i ^ bit) for i in range(size)])  39.3 us
    ppermute x16, waiting for transfers between devices, turn(): lax.ppermute(block, axis, [(i, (i + step) % RING) for i in range(RING)])  37.4 us
    ppermute x16, waiting for transfers between devices, swap(): return lax.ppermute(block, axis, [(i, i ^ bit) for i in range(size)])  34.9 us
    ppermute x16, starting transfers between devices, turn(): lax.ppermute(block, axis, [(i, (i + step) % RING) for i in range(RING)])  21.6 us
    dot_general x5, matrix products, cross_product(): lax.dot_general(left, right, (((0,), (0,)), ((), ())), preferred_element_...  13.4 us
    dot_general x3, matrix products, matmul(): return jnp.dot(left, right, preferred_element_type=jnp.float32)  13 us
    pallas_call x7, Pallas kernels, copies(): pl.pallas_call(kernel, out_shape=[jax.ShapeDtypeStruct(shape, dtype) for...  12.1 us
    select_n x6, other arithmetic, join(): jnp.where(bit == 0, jnp.concatenate([mine, other]), jnp.concatenate([othe...  6.3 us
  transfers between devices with their start and end apart: 35, of which 17 were waited for; matrix products, arithmetic and copies ran while one was open for 18% of the time, Pallas kernels for 5%

profile of v1, /device:TPU:1, one launch (start us, length us, event | category | flops | bytes accessed | tf_op | source)
XLA Modules:
  0.0 230.1 jit_solution(9243211773538445495)
XLA Ops:
  7.2 7.8 %collective-permute-start = (bf16[64,1792]{1,0:T(8,128)(2,1)}, bf16[64,1792]{1,0:T(8,128)(2,1)S(1)}, u32[]{:S(2)}, u32[]{:S(2)}) collective-permute-start(bf16[64,1792]{1,0:T(8,128)(2,1)} %refs_0_.1), channel_id=1, source_target_pairs={{0,8},{8,0},{1,9},{9,1},{2,10},{10,2},{3,11},{11,3},{4,12},{12,4},... | collective-permute-start | bytes 688136 | tf_op jit(solution)/shard_map/ppermute | solution.py:22
  19.6 5.3 %collective-permute-done.1 = bf16[64,512]{1,0:T(8,128)(2,1)S(1)} collective-permute-done((bf16[64,512]{1,0:T(8,128)(2,1)}, bf16[64,512]{1,0:T(8,128)(2,1)S(1)}, u32[]{:S(2)}, u32[]{:S(2)}) %collective-permute-start.1) | collective-permute-done | bytes 65568 | tf_op jit(solution)/shard_map/ppermute | solution.py:22
  25.5 3.6 %collective-permute-start.4 = (bf16[1,4,64,576]{3,2,1,0:T(8,128)(2,1)S(1)}, bf16[1,4,64,576]{3,2,1,0:T(8,128)(2,1)}, u32[]{:S(2)}, u32[]{:S(2)}) collective-permute-start(bf16[1,4,64,576]{3,2,1,0:T(8,128)(2,1)S(1)} %maximum_bitcast_fusion), channel_id=1, source_target_pairs={{0,2},{2,0},{4,6},{6,4},{1,3},{3,1},{5,7},{7,5},{8,10},{10,8},{12,... | collective-permute-start | bytes 884744 | tf_op jit(solution)/shard_map/ppermute | solution.py:22
  29.1 2.7 %collective-permute-start.5 = (bf16[64,1792]{1,0:T(8,128)(2,1)S(1)}, bf16[64,1792]{1,0:T(8,128)(2,1)S(1)}, u32[]{:S(2)}, u32[]{:S(2)}) collective-permute-start(bf16[64,1792]{1,0:T(8,128)(2,1)S(1)} %collective-permute-done.refs_0_), channel_id=1, source_target_pairs={{0,48},{16,0},{32,16},{48,32},{1,49},{17,1},{33,17},{49,33},{2,50}... | collective-permute-start | bytes 688136 | tf_op jit(solution)/shard_map/ppermute | solution.py:26
  36.3 3.5 %collective-permute-done.6.refs_0_.refs_4_ = bf16[64,1792]{1,0:T(8,128)(2,1)S(1)} collective-permute-done((bf16[64,1792]{1,0:T(8,128)(2,1)S(1)}, bf16[64,1792]{1,0:T(8,128)(2,1)S(1)}, u32[]{:S(2)}, u32[]{:S(2)}) %collective-permute-start.6) | collective-permute-done | bytes 229408 | tf_op jit(solution)/shard_map/ppermute | solution.py:26
  54.6 21.8 %collective-permute-done.14.refs_0_.refs_9_ = bf16[256,1792]{1,0:T(8,128)(2,1)} collective-permute-done((bf16[256,1792]{1,0:T(8,128)(2,1)S(1)}, bf16[256,1792]{1,0:T(8,128)(2,1)}, u32[]{:S(2)}, u32[]{:S(2)}) %collective-permute-start.14) | collective-permute-done | bytes 917536 | tf_op jit(solution)/shard_map/ppermute | solution.py:26
  81.1 2.8 %collective-permute-done.7 = bf16[2,4,64,576]{3,2,1,0:T(8,128)(2,1)} collective-permute-done((bf16[2,4,64,576]{3,2,1,0:T(8,128)(2,1)}, bf16[2,4,64,576]{3,2,1,0:T(8,128)(2,1)}, u32[]{:S(2)}, u32[]{:S(2)}) %collective-permute-start.7) | collective-permute-done | bytes 589856 | tf_op jit(solution)/shard_map/ppermute | solution.py:22
  93.4 8.3 %collective-permute-done.21.refs_7_ = bf16[128,1792]{1,0:T(8,128)(2,1)} collective-permute-done((bf16[128,1792]{1,0:T(8,128)(2,1)}, bf16[128,1792]{1,0:T(8,128)(2,1)}, u32[]{:S(2)}, u32[]{:S(2)}) %collective-permute-start.21) | collective-permute-done | bytes 458784 | tf_op jit(solution)/shard_map/ppermute | solution.py:26
  103.8 4.7 %shard_map.73 = bf16[2048,1792]{1,0:T(8,128)(2,1)S(1)} custom-call(bf16[256,1792]{1,0:T(8,128)(2,1)S(1)} %shard_map.68.refs_0_, bf16[256,1792]{1,0:T(8,128)(2,1)} %collective-permute-done.13.refs_1_, bf16[128,1792]{1,0:T(8,128)(2,1)} %collective-permute-done.19.refs_2_, bf16[128,1792]{1,0:T(8,128)(2,1)} %collective-permute-done.20.refs_3_, ...), custom_call_target="tpu_custom_call" | custom-call | bytes 14680064 | tf_op jit(solution)/shard_map/pallas_call | solution.py:49
  108.5 3.7 %maximum_select_fusion.1 = bf16[4,2,2,64,576]{4,3,2,1,0:T(8,128)(2,1)} fusion(bf16[4,1,2,64,576]{4,3,2,1,0:T(8,128)(2,1)} %bitcast.9, bf16[4,1,2,64,576]{4,3,2,1,0:T(8,128)(2,1)S(1)} %copy-done.13, pred[]{:T(512)S(6)} %eq.12), kind=kLoop, calls=%fused_computation.7 | loop fusion | flops 1769472 | bytes 2359297 | tf_op jit(solution)/shard_map/jit(_where)/select_n | solution.py:190
  114.9 3.4 %fusion.13 = (bf16[1024,1792]{1,0:T(8,128)(2,1)}, bf16[1024,1792]{1,0:T(8,128)(2,1)}) fusion(bf16[2048,1792]{1,0:T(8,128)(2,1)S(1)} %shard_map.73), kind=kLoop, calls=%fused_computation.48 | loop fusion | bytes 14680064 | tf_op jit(solution)/shard_map/slice | solution.py:202
  118.3 2.7 %fusion.3 = f32[128,512]{1,0:T(8,128)} fusion(bf16[2048,512]{1,0:T(8,128)(2,1)} %all-gather.4.cloned.1.call-done, bf16[64,2048]{1,0:T(8,128)(2,1)S(1)} %collective-permute-done.17, bf16[64,2048]{1,0:T(8,128)(2,1)S(1)} %copy_bitcast_fusion), kind=kOutput, calls=%fused_computation.16 | convolution fusion | flops 269484032 | bytes 2883584 | tf_op jit(solution)/shard_map/dot_general | solution.py:136
  121.1 5.2 %fusion.16 = f32[1024,448]{0,1:T(8,128)} fusion(bf16[1024,1792]{1,0:T(8,128)(2,1)} %get-tuple-element.45, bf16[1792,448]{0,1:T(8,128)(2,1)S(1)} %copy-done), kind=kOutput, calls=%fused_computation.51 | convolution fusion | flops 1644167168 | bytes 7110656 | tf_op jit(solution)/shard_map/dot_general | solution.py:136
  126.9 4.5 %collective-permute-start.18 = (f32[128,512]{1,0:T(8,128)}, f32[128,512]{1,0:T(8,128)}, u32[]{:S(2)}, u32[]{:S(2)}) collective-permute-start(f32[128,512]{1,0:T(8,128)} %fusion.3), channel_id=1, source_target_pairs={{0,8},{8,0},{1,9},{9,1},{2,10},{10,2},{3,11},{11,3},{4,12},{12,4},... | collective-permute-start | bytes 786440 | tf_op jit(solution)/shard_map/ppermute | solution.py:22
  131.4 5.1 %abs_reduce_fusion = (f32[]{:T(128)}, f32[1024,448]{0,1:T(8,128)S(1)}) fusion(f32[1024,448]{0,1:T(8,128)} %collective-permute-done.23, bf16[1024,1792]{1,0:T(8,128)(2,1)} %get-tuple-element.46, bf16[1792,448]{0,1:T(8,128)(2,1)S(1)} %copy-done), kind=kOutput, calls=%fused_computation.3 | convolution fusion | flops 1645543424 | bytes 8945668 | tf_op jit(solution)/shard_map/dot_general | solution.py:136
  143.0 5.6 %all-to-all-start = ((bf16[16,64,576]{2,1,0:T(8,128)(2,1)}), bf16[16,64,576]{2,1,0:T(8,128)(2,1)S(1)}, u32[]{:S(2)}, u32[]{:S(2)}) async-start(bf16[16,64,576]{2,1,0:T(8,128)(2,1)} %bitcast.10), calls=%async_computation | async-start | bytes 2621440 | tf_op jit(solution)/shard_map/all_to_all | solution.py:215
  148.6 4.1 %collective-permute-start.24 = (f16[512,448]{0,1:T(8,128)(2,1)}, f16[512,448]{0,1:T(8,128)(2,1)}, u32[]{:S(2)}, u32[]{:S(2)}) collective-permute-start(f16[512,448]{0,1:T(8,128)(2,1)} %multiply_convert_fusion), channel_id=1, source_target_pairs={{0,2},{2,0},{4,6},{6,4},{1,3},{3,1},{5,7},{7,5},{8,10},{10,8},{12,... | collective-permute-start | bytes 1376264 | tf_op jit(solution)/shard_map/ppermute | solution.py:22
  152.9 9.3 %collective-permute-done.25 = f32[8,128]{1,0:T(8,128)S(1)} collective-permute-done((f32[8,128]{1,0:T(8,128)S(1)}, f32[8,128]{1,0:T(8,128)S(1)}, u32[]{:S(2)}, u32[]{:S(2)}) %collective-permute-start.25) | collective-permute-done | bytes 4128 | tf_op jit(solution)/shard_map/ppermute | solution.py:22
  167.1 4.5 %collective-permute-start.28 = (bf16[1024,576]{0,1:T(8,128)(2,1)S(1)}, bf16[1024,576]{0,1:T(8,128)(2,1)}, u32[]{:S(2)}, u32[]{:S(2)}) collective-permute-start(bf16[1024,576]{0,1:T(8,128)(2,1)S(1)} %copy.10), channel_id=1, source_target_pairs={{0,1},{1,0},{2,3},{3,2},{4,5},{5,4},{6,7},{7,6},{8,9},{9,8},{10,11... | collective-permute-start | bytes 3538952 | tf_op jit(solution)/shard_map/ppermute | solution.py:22
  171.6 10.1 %collective-permute-start.27 = (f32[8,128]{1,0:T(8,128)S(1)}, f32[8,128]{1,0:T(8,128)S(1)}, u32[]{:S(2)}, u32[]{:S(2)}) collective-permute-start(f32[8,128]{1,0:T(8,128)S(1)} %broadcast_in_dim.11), channel_id=1, source_target_pairs={{0,4},{2,6},{4,0},{6,2},{1,5},{3,7},{5,1},{7,3},{8,12},{10,14},{12... | collective-permute-start | bytes 12296 | tf_op jit(solution)/shard_map/ppermute | solution.py:22
  183.7 10.3 %collective-permute-done.26 = f16[256,448]{0,1:T(8,128)(2,1)S(1)} collective-permute-done((f16[256,448]{0,1:T(8,128)(2,1)S(1)}, f16[256,448]{0,1:T(8,128)(2,1)S(1)}, u32[]{:S(2)}, u32[]{:S(2)}) %collective-permute-start.26) | collective-permute-done | bytes 229408 | tf_op jit(solution)/shard_map/ppermute | solution.py:22
  195.4 8.4 %convolution_multiply_fusion = f32[1792,448]{0,1:T(8,128)} fusion(bf16[2048,1792]{1,0:T(8,128)(2,1)} %copy-done.2, bf16[2048,576]{1,0:T(8,128)(2,1)S(1)} %pad_maximum_fusion), kind=kOutput, calls=%fused_computation | convolution fusion | flops 3289137152 | bytes 12648448 | tf_op jit(solution)/shard_map/dot_general | solution.py:140
  206.3 4.0 %all-gather.6.cloned.1.call-done = bf16[2048,1024]{1,0:T(8,128)(2,1)} async-done(((bf16[128,1024]{1,0:T(8,128)(2,1)}), bf16[2048,1024]{1,0:T(8,128)(2,1)}) %all-gather.6.cloned.1.call-update) | async-done | bytes 4194320 | tf_op jit(solution)/shard_map/all_gather | solution.py:213
  210.3 2.7 %fusion.14 = (bf16[16,1,64,512]{3,2,1,0:T(8,128)(2,1)S(1)}, bf16[16,1,64,512]{3,2,1,0:T(8,128)(2,1)S(1)}, bf16[16,1,64,512]{3,2,1,0:T(8,128)(2,1)S(1)}, bf16[16,1,64,512]{3,2,1,0:T(8,128)(2,1)S(1)}) fusion(bf16[16,2,64,1024]{3,2,1,0:T(8,128)(2,1)} %bitcast.46), kind=kLoop, calls=%fused_computation.49 | loop fusion | bytes 8388608 | tf_op jit(solution)/shard_map/slice | solution.py:234
  (129 shorter events, 68.6 us)
Async XLA Ops:
  7.2 111.1 %all-gather.4.cloned.1.call-start = ((), (), s32[]{:S(2)}) async-start(), calls=%async_computation.1 | async-start | bytes 2228224 | tf_op jit(solution)/shard_map/all_gather | solution.py:155
  7.2 17.7 %collective-permute-start = (bf16[64,1792]{1,0:T(8,128)(2,1)}, bf16[64,1792]{1,0:T(8,128)(2,1)S(1)}, u32[]{:S(2)}, u32[]{:S(2)}) collective-permute-start(bf16[64,1792]{1,0:T(8,128)(2,1)} %refs_0_.1), channel_id=1, source_target_pairs={{0,8},{8,0},{1,9},{9,1},{2,10},{10,2},{3,11},{11,3},{4,12},{12,4},... | collective-permute-start | bytes 688136 | tf_op jit(solution)/shard_map/ppermute | solution.py:22
  17.7 192.6 %all-gather.6.cloned.1.call-start = ((), (), s32[]{:S(2)}) async-start(), calls=%async_computation.2 | async-start | bytes 4456448 | tf_op jit(solution)/shard_map/all_gather | solution.py:213
  25.5 17.3 %collective-permute-start.4 = (bf16[1,4,64,576]{3,2,1,0:T(8,128)(2,1)S(1)}, bf16[1,4,64,576]{3,2,1,0:T(8,128)(2,1)}, u32[]{:S(2)}, u32[]{:S(2)}) collective-permute-start(bf16[1,4,64,576]{3,2,1,0:T(8,128)(2,1)S(1)} %maximum_bitcast_fusion), channel_id=1, source_target_pairs={{0,2},{2,0},{4,6},{6,4},{1,3},{3,1},{5,7},{7,5},{8,10},{10,8},{12,... | collective-permute-start | bytes 884744 | tf_op jit(solution)/shard_map/ppermute | solution.py:22
  32.2 12.8 %collective-permute-start.8 = (bf16[32,1792]{1,0:T(8,128)(2,1)S(1)}, bf16[32,1792]{1,0:T(8,128)(2,1)S(1)}, u32[]{:S(2)}, u32[]{:S(2)}) collective-permute-start(bf16[32,1792]{1,0:T(8,128)(2,1)S(1)} %get-tuple-element.32), channel_id=1, source_target_pairs={{0,64},{64,128},{128,192},{192,0},{1,65},{65,129},{129,193},{193,1... | collective-permute-start | bytes 344072 | tf_op jit(solution)/shard_map/ppermute | solution.py:26
  34.0 11.0 %collective-permute-start.9 = (bf16[32,1792]{1,0:T(8,128)(2,1)S(1)}, bf16[32,1792]{1,0:T(8,128)(2,1)S(1)}, u32[]{:S(2)}, u32[]{:S(2)}) collective-permute-start(bf16[32,1792]{1,0:T(8,128)(2,1)S(1)} %get-tuple-element.33), channel_id=1, source_target_pairs={{0,192},{64,0},{128,64},{192,128},{1,193},{65,1},{129,65},{193,129... | collective-permute-start | bytes 344072 | tf_op jit(solution)/shard_map/ppermute | solution.py:26
  47.6 28.8 %collective-permute-start.14 = (bf16[256,1792]{1,0:T(8,128)(2,1)S(1)}, bf16[256,1792]{1,0:T(8,128)(2,1)}, u32[]{:S(2)}, u32[]{:S(2)}) collective-permute-start(bf16[256,1792]{1,0:T(8,128)(2,1)S(1)} %shard_map.70.refs_5_), channel_id=1, source_target_pairs={{0,64},{64,128},{128,192},{192,0},{1,65},{65,129},{129,193},{193,1... | collective-permute-start | bytes 2752520 | tf_op jit(solution)/shard_map/ppermute | solution.py:26
  49.6 27.0 %collective-permute-start.15 = (bf16[256,1792]{1,0:T(8,128)(2,1)S(1)}, bf16[256,1792]{1,0:T(8,128)(2,1)}, u32[]{:S(2)}, u32[]{:S(2)}) collective-permute-start(bf16[256,1792]{1,0:T(8,128)(2,1)S(1)} %shard_map.70.refs_5_), channel_id=1, source_target_pairs={{0,192},{64,0},{128,64},{192,128},{1,193},{65,1},{129,65},{193,129... | collective-permute-start | bytes 2752520 | tf_op jit(solution)/shard_map/ppermute | solution.py:26
  50.4 28.3 %collective-permute-start.12 = (bf16[256,1792]{1,0:T(8,128)(2,1)S(1)}, bf16[256,1792]{1,0:T(8,128)(2,1)}, u32[]{:S(2)}, u32[]{:S(2)}) collective-permute-start(bf16[256,1792]{1,0:T(8,128)(2,1)S(1)} %shard_map.68.refs_0_), channel_id=1, source_target_pairs={{0,16},{16,32},{32,48},{48,0},{1,17},{17,33},{33,49},{49,1},{2,18}... | collective-permute-start | bytes 2752520 | tf_op jit(solution)/shard_map/ppermute | solution.py:26
  50.4 28.5 %collective-permute-start.13 = (bf16[256,1792]{1,0:T(8,128)(2,1)S(1)}, bf16[256,1792]{1,0:T(8,128)(2,1)}, u32[]{:S(2)}, u32[]{:S(2)}) collective-permute-start(bf16[256,1792]{1,0:T(8,128)(2,1)S(1)} %shard_map.68.refs_0_), channel_id=1, source_target_pairs={{0,48},{16,0},{32,16},{48,32},{1,49},{17,1},{33,17},{49,33},{2,50}... | collective-permute-start | bytes 2752520 | tf_op jit(solution)/shard_map/ppermute | solution.py:26
  53.1 30.7 %collective-permute-start.7 = (bf16[2,4,64,576]{3,2,1,0:T(8,128)(2,1)}, bf16[2,4,64,576]{3,2,1,0:T(8,128)(2,1)}, u32[]{:S(2)}, u32[]{:S(2)}) collective-permute-start(bf16[2,4,64,576]{3,2,1,0:T(8,128)(2,1)} %maximum_select_fusion.4), channel_id=1, source_target_pairs={{0,4},{2,6},{4,0},{6,2},{1,5},{3,7},{5,1},{7,3},{8,12},{10,14},{12... | collective-permute-start | bytes 1769480 | tf_op jit(solution)/shard_map/ppermute | solution.py:22
  86.7 21.8 %collective-permute-start.16 = (bf16[4,2,64,576]{3,2,1,0:T(8,128)(2,1)}, bf16[4,2,64,576]{3,2,1,0:T(8,128)(2,1)}, u32[]{:S(2)}, u32[]{:S(2)}) collective-permute-start(bf16[4,2,64,576]{3,2,1,0:T(8,128)(2,1)} %get-tuple-element.66), channel_id=1, source_target_pairs={{0,1},{1,0},{2,3},{3,2},{4,5},{5,4},{6,7},{7,6},{8,9},{9,8},{10,11... | collective-permute-start | bytes 1769480 | tf_op jit(solution)/shard_map/ppermute | solution.py:22
  88.0 13.7 %collective-permute-start.21 = (bf16[128,1792]{1,0:T(8,128)(2,1)}, bf16[128,1792]{1,0:T(8,128)(2,1)}, u32[]{:S(2)}, u32[]{:S(2)}) collective-permute-start(bf16[128,1792]{1,0:T(8,128)(2,1)} %get-tuple-element.42), channel_id=1, source_target_pairs={{0,64},{64,128},{128,192},{192,0},{1,65},{65,129},{129,193},{193,1... | collective-permute-start | bytes 1376264 | tf_op jit(solution)/shard_map/ppermute | solution.py:26
  89.4 12.3 %collective-permute-start.22 = (bf16[128,1792]{1,0:T(8,128)(2,1)}, bf16[128,1792]{1,0:T(8,128)(2,1)}, u32[]{:S(2)}, u32[]{:S(2)}) collective-permute-start(bf16[128,1792]{1,0:T(8,128)(2,1)} %get-tuple-element.43), channel_id=1, source_target_pairs={{0,192},{64,0},{128,64},{192,128},{1,193},{65,1},{129,65},{193,129... | collective-permute-start | bytes 1376264 | tf_op jit(solution)/shard_map/ppermute | solution.py:26
  90.7 13.0 %collective-permute-start.19 = (bf16[128,1792]{1,0:T(8,128)(2,1)}, bf16[128,1792]{1,0:T(8,128)(2,1)}, u32[]{:S(2)}, u32[]{:S(2)}) collective-permute-start(bf16[128,1792]{1,0:T(8,128)(2,1)} %get-tuple-element.39), channel_id=1, source_target_pairs={{0,16},{16,32},{32,48},{48,0},{1,17},{17,33},{33,49},{49,1},{2,18}... | collective-permute-start | bytes 1376264 | tf_op jit(solution)/shard_map/ppermute | solution.py:26
  90.7 13.0 %collective-permute-start.20 = (bf16[128,1792]{1,0:T(8,128)(2,1)}, bf16[128,1792]{1,0:T(8,128)(2,1)}, u32[]{:S(2)}, u32[]{:S(2)}) collective-permute-start(bf16[128,1792]{1,0:T(8,128)(2,1)} %get-tuple-element.40), channel_id=1, source_target_pairs={{0,48},{16,0},{32,16},{48,32},{1,49},{17,1},{33,17},{49,33},{2,50}... | collective-permute-start | bytes 1376264 | tf_op jit(solution)/shard_map/ppermute | solution.py:26
  126.9 11.6 %collective-permute-start.18 = (f32[128,512]{1,0:T(8,128)}, f32[128,512]{1,0:T(8,128)}, u32[]{:S(2)}, u32[]{:S(2)}) collective-permute-start(f32[128,512]{1,0:T(8,128)} %fusion.3), channel_id=1, source_target_pairs={{0,8},{8,0},{1,9},{9,1},{2,10},{10,2},{3,11},{11,3},{4,12},{12,4},... | collective-permute-start | bytes 786440 | tf_op jit(solution)/shard_map/ppermute | solution.py:22
  143.0 23.4 %all-to-all-start = ((bf16[16,64,576]{2,1,0:T(8,128)(2,1)}), bf16[16,64,576]{2,1,0:T(8,128)(2,1)S(1)}, u32[]{:S(2)}, u32[]{:S(2)}) async-start(bf16[16,64,576]{2,1,0:T(8,128)(2,1)} %bitcast.10), calls=%async_computation | async-start | bytes 2621440 | tf_op jit(solution)/shard_map/all_to_all | solution.py:215
  148.6 15.5 %collective-permute-start.24 = (f16[512,448]{0,1:T(8,128)(2,1)}, f16[512,448]{0,1:T(8,128)(2,1)}, u32[]{:S(2)}, u32[]{:S(2)}) collective-permute-start(f16[512,448]{0,1:T(8,128)(2,1)} %multiply_convert_fusion), channel_id=1, source_target_pairs={{0,2},{2,0},{4,6},{6,4},{1,3},{3,1},{5,7},{7,5},{8,10},{10,8},{12,... | collective-permute-start | bytes 1376264 | tf_op jit(solution)/shard_map/ppermute | solution.py:22
  167.1 14.6 %collective-permute-start.28 = (bf16[1024,576]{0,1:T(8,128)(2,1)S(1)}, bf16[1024,576]{0,1:T(8,128)(2,1)}, u32[]{:S(2)}, u32[]{:S(2)}) collective-permute-start(bf16[1024,576]{0,1:T(8,128)(2,1)S(1)} %copy.10), channel_id=1, source_target_pairs={{0,1},{1,0},{2,3},{3,2},{4,5},{5,4},{6,7},{7,6},{8,9},{9,8},{10,11... | collective-permute-start | bytes 3538952 | tf_op jit(solution)/shard_map/ppermute | solution.py:22
  171.6 12.1 %collective-permute-start.27 = (f32[8,128]{1,0:T(8,128)S(1)}, f32[8,128]{1,0:T(8,128)S(1)}, u32[]{:S(2)}, u32[]{:S(2)}) collective-permute-start(f32[8,128]{1,0:T(8,128)S(1)} %broadcast_in_dim.11), channel_id=1, source_target_pairs={{0,4},{2,6},{4,0},{6,2},{1,5},{3,7},{5,1},{7,3},{8,12},{10,14},{12... | collective-permute-start | bytes 12296 | tf_op jit(solution)/shard_map/ppermute | solution.py:22
  181.7 12.3 %collective-permute-start.26 = (f16[256,448]{0,1:T(8,128)(2,1)S(1)}, f16[256,448]{0,1:T(8,128)(2,1)S(1)}, u32[]{:S(2)}, u32[]{:S(2)}) collective-permute-start(f16[256,448]{0,1:T(8,128)(2,1)S(1)} %multiply_convert_fusion.2), channel_id=1, source_target_pairs={{0,4},{2,6},{4,0},{6,2},{1,5},{3,7},{5,1},{7,3},{8,12},{10,14},{12... | collective-permute-start | bytes 688136 | tf_op jit(solution)/shard_map/ppermute | solution.py:22
  195.3 10.8 %collective-permute-start.29 = (bf16[256,448]{0,1:T(8,128)(2,1)S(1)}, bf16[256,448]{0,1:T(8,128)(2,1)S(1)}, u32[]{:S(2)}, u32[]{:S(2)}) collective-permute-start(bf16[256,448]{0,1:T(8,128)(2,1)S(1)} %multiply_convert_fusion.1), channel_id=1, source_target_pairs={{0,4},{2,6},{4,0},{6,2},{1,5},{3,7},{5,1},{7,3},{8,12},{10,14},{12... | collective-permute-start | bytes 688136 | tf_op jit(solution)/shard_map/ppermute | solution.py:22
  206.2 11.8 %collective-permute-start.30 = (bf16[512,448]{0,1:T(8,128)(2,1)S(1)}, bf16[512,448]{0,1:T(8,128)(2,1)S(1)}, u32[]{:S(2)}, u32[]{:S(2)}) collective-permute-start(bf16[512,448]{0,1:T(8,128)(2,1)S(1)} %maximum_select_fusion.5), channel_id=1, source_target_pairs={{0,2},{2,0},{4,6},{6,4},{1,3},{3,1},{5,7},{7,5},{8,10},{10,8},{12,... | collective-permute-start | bytes 1376264 | tf_op jit(solution)/shard_map/ppermute | solution.py:22
  (28 other events, 325.9 us)
Sparse Core Ops, SparseCore 0:
  17.8 58.3 all-gather.3
  143.1 67.0 all-gather.5
